TPU v7x, 32 devices: a whole 2x2x4 slice. The times are simulated.
32 devices in a mesh: seq: 16 (over z, y, core), head: 2 (over x).
Axes of the slice: x: 2, y: 2, z: 4, core: 2. Of those that a mesh axis runs over, the one named last changes fastest.
Arguments:
- query_main: bfloat16 [512, 2048], P(('seq', 'head')), may hold values from -5 to 5
- key_main: bfloat16 [512, 2048], P(('seq', 'head')), may hold values from -5 to 5
- value_main: bfloat16 [512, 2048], P(('seq', 'head')), may hold values from -5 to 5
- query_tan: bfloat16 [512, 2048], P(('seq', 'head')), may hold values from -5 to 5
- key_tan: bfloat16 [512, 2048], P(('seq', 'head')), may hold values from -5 to 5
- value_tan: bfloat16 [512, 2048], P(('seq', 'head')), may hold values from -5 to 5
- positions: int32 [512], P(('seq', 'head')), may hold values from 0 to 1073741823, as said below
Outputs:
- attended: bfloat16 [512, 2048], P(('seq', 'head'))
- attended_tan: bfloat16 [512, 2048], P(('seq', 'head'))
Inputs may be any that keep to these rules, and one draw needn't show every extreme that they name: `positions`: 512 distinct values.
All inputs are finite; a program needn't handle non-finite values.
Results may differ from a plain program's by a relative error of at most 0.035.
Values may be sent and summed in bfloat16 or wider, within the bound.
No kernel may reach another device: no remote copies, remote signals or barrier semaphores. Data moves between devices by JAX's collectives and lax.ppermute only.
A program may use at most 128 MiB of HBM per device.

v0:
```python
import functools
import math

import jax
import jax.numpy as jnp
from jax import lax
from jax.experimental import pallas as pl
from jax.experimental.pallas import tpu as pltpu
from jax.sharding import PartitionSpec as P

HEADS = 16
HEAD_DIM = 128
LOG2_E = math.log2(math.e)
AXES = ("seq", "head")
TILE = 8
MIDDLE = 11
ARRAYS = 6
PIECES = 4


def plan(mesh):
    heads_axis = mesh.shape["head"]
    peers = mesh.shape["seq"] * heads_axis // HEADS
    assert mesh.shape["seq"] % peers == 0

    def flat(peer, head):
        member = head ^ MIDDLE
        return (member // heads_axis * peers + peer) * heads_axis + member % heads_axis

    return [[flat(peer, head) for head in range(HEADS)] for peer in range(peers)]


def as_tiles(array):
    rows, columns = array.shape
    return array.reshape(rows // TILE, TILE, columns // HEAD_DIM, HEAD_DIM).transpose(0, 2, 1, 3)


def from_tiles(tiles):
    row_tiles, heads = tiles.shape[:2]
    return tiles.transpose(0, 2, 1, 3).reshape(row_tiles * TILE, heads * HEAD_DIM)


def pack_kernel(positions, *refs):
    arrays, (out, here, sems) = refs[:ARRAYS], refs[ARRAYS:]
    row_tiles = arrays[0].shape[0]
    last = ARRAYS * row_tiles
    load = pltpu.make_async_copy(positions, here, sems.at[last])
    load.start()
    copies = []
    for at, array in enumerate(arrays):
        for tile in range(row_tiles):
            slot = at * row_tiles + tile
            copies.append(pltpu.make_async_copy(array.at[tile], out.at[:, slot], sems.at[slot]))
            copies[-1].start()
    token = lax.broadcasted_iota(jnp.int32, (TILE, HEAD_DIM), 0)
    lane = lax.broadcasted_iota(jnp.int32, (TILE, HEAD_DIM), 1)
    token = token + lane // (HEAD_DIM // row_tiles) * TILE
    place = jnp.zeros((TILE, HEAD_DIM), jnp.int32)
    load.wait()
    for t in range(row_tiles * TILE):
        place = jnp.where(token == t, here[t], place)
    place = lax.shift_right_logical(place, lane % PIECES * 8) & 255
    place = place.astype(jnp.float32).astype(jnp.bfloat16)
    for head in range(HEADS):
        out[head, last] = place
    for copy in copies:
        copy.wait()


def pack(positions, arrays):
    tiles = [as_tiles(array) for array in arrays]
    slots = ARRAYS * tiles[0].shape[0] + 1
    packed = pl.pallas_call(
        pack_kernel,
        out_shape=pltpu.VMEM((HEADS, slots, TILE, HEAD_DIM), jnp.bfloat16),
        in_specs=[pl.BlockSpec(memory_space=pltpu.HBM)] * (1 + ARRAYS),
        out_specs=pl.BlockSpec(memory_space=pltpu.VMEM),
        scratch_shapes=[
            pltpu.SMEM(positions.shape, jnp.int32),
            pltpu.SemaphoreType.DMA((slots,)),
        ],
        compiler_params=pltpu.CompilerParams(vmem_limit_bytes=56 * 2**20),
        name="pack",
    )(positions, *tiles)
    return packed.reshape(HEADS, slots * TILE, HEAD_DIM)


def without_queries(messages, rows):
    heads, length, lanes = messages.shape

    def kernel(whole, out):
        out[...] = whole[:, 2 * rows :, :]

    return pl.pallas_call(
        kernel,
        out_shape=jax.ShapeDtypeStruct((heads, length - 2 * rows, lanes), messages.dtype),
        in_specs=[pl.BlockSpec(memory_space=pltpu.VMEM)],
        out_specs=pl.BlockSpec(memory_space=pltpu.VMEM),
        compiler_params=pltpu.CompilerParams(vmem_limit_bytes=4 * 2**20),
        name="shared",
    )(messages)


def dot(a, b, contract):
    return lax.dot_general(a, b, (contract, ((), ())), preferred_element_type=jnp.float32)


def order_of(pair):
    high, low = pair
    return high.astype(jnp.int32) * 65536 + low.astype(jnp.int32)


def attention_kernel(rows, *refs):
    blocks, out = refs[:-1], refs[-1]
    own = blocks[0]
    count = HEADS * rows
    scale = HEAD_DIM ** (-0.5)
    lanes = HEAD_DIM * TILE // rows

    def part(ref, at):
        return ref[:, at * rows : (at + 1) * rows, :].reshape(count, HEAD_DIM)

    def key_part(ref, at):
        return part(ref, at + 2 if ref is own else at)

    def places(ref):
        packed = ref[:, ref.shape[1] - TILE :, :].astype(jnp.float32)
        lane = lax.broadcasted_iota(jnp.int32, packed.shape, 2)
        parts = [jnp.where(lane // lanes == at, packed, 0.0) for at in range(rows // TILE)]
        return jnp.stack(parts, axis=1).reshape(count, HEAD_DIM).astype(jnp.bfloat16)

    def weights(shape, axis, first):
        at = lax.broadcasted_iota(jnp.int32, shape, axis) % lanes
        chosen = jnp.where(at == first, 1.0, jnp.where(at == first + 1, 256.0, 0.0))
        return chosen.astype(jnp.bfloat16)

    queries = part(own, 0)
    query_pair = jnp.concatenate([part(own, 1), queries], axis=1)
    own_order = places(own)
    across = (HEAD_DIM, HEAD_DIM)
    query_order = order_of([dot(own_order, weights(across, 0, first), ((1,), (0,))) for first in (2, 0)])
    state = None
    for start in range(0, len(blocks), 2):
        group = blocks[start : start + 2]

        def keyed(at):
            return jnp.concatenate([key_part(ref, at) for ref in group], axis=0)

        keys, values, key_dot, value_dot = [keyed(at) for at in range(4)]
        order = jnp.concatenate([places(ref) for ref in group], axis=0)
        width = keys.shape[0]
        down = (8, HEAD_DIM)
        key_order = order_of([dot(weights(down, 1, first), order, ((1,), (1,))) for first in (2, 0)])
        wide_order = jnp.concatenate([query_order] * (width // HEAD_DIM), axis=1)
        visible = key_order[:1] <= wide_order
        scores = dot(queries, keys, ((1,), (1,)))
        scores = jnp.where(visible, scores, -1e30)
        key_pair = jnp.concatenate([keys, key_dot], axis=1)
        score_tan = dot(query_pair, key_pair, ((1,), (1,)))
        new_max = jnp.max(scores, axis=1, keepdims=True)
        if state is not None:
            new_max = jnp.maximum(new_max, state[0])
        expo = jnp.exp2((scores - new_max) * (scale * LOG2_E))
        total = jnp.sum(expo, axis=1, keepdims=True)
        both = dot(expo.astype(jnp.bfloat16), jnp.concatenate([values, value_dot], axis=1), ((1,), (0,)))
        summed = jnp.concatenate([values, jnp.ones_like(values)], axis=1)
        moved = dot((expo * score_tan).astype(jnp.bfloat16), summed, ((1,), (0,)))
        if state is not None:
            shrink = jnp.exp2((state[0] - new_max) * (scale * LOG2_E))
            total, both, moved = [new + old * shrink for new, old in zip((total, both, moved), state[1:])]
        state = (new_max, total, both, moved)
    _, total, both, moved = state
    inverse = 1.0 / total
    mixed = both[:, :HEAD_DIM] * inverse
    weighted, mass = moved[:, :HEAD_DIM], moved[:, HEAD_DIM:]
    tangent = both[:, HEAD_DIM:] * inverse + (weighted - mass * mixed) * (inverse * scale)
    out[:, :rows, :] = mixed.astype(jnp.bfloat16).reshape(HEADS, rows, HEAD_DIM)
    out[:, rows:, :] = tangent.astype(jnp.bfloat16).reshape(HEADS, rows, HEAD_DIM)


def attention(rows, blocks):
    return pl.pallas_call(
        functools.partial(attention_kernel, rows),
        out_shape=jax.ShapeDtypeStruct((HEADS, 2 * rows, HEAD_DIM), jnp.bfloat16),
        in_specs=[pl.BlockSpec(memory_space=pltpu.VMEM)] * len(blocks),
        out_specs=pl.BlockSpec(memory_space=pltpu.VMEM),
        compiler_params=pltpu.CompilerParams(vmem_limit_bytes=(8 + len(blocks)) * 2**20),
        name="attention",
    )(*blocks)


def unpack_kernel(packed, *refs):
    outs, sems = refs[:2], refs[2]
    row_tiles = outs[0].shape[0]
    copies = []
    for at, out in enumerate(outs):
        for tile in range(row_tiles):
            slot = at * row_tiles + tile
            copies.append(pltpu.make_async_copy(packed.at[:, slot], out.at[tile], sems.at[slot]))
            copies[-1].start()
    for copy in copies:
        copy.wait()


def unpack(packed):
    slots = packed.shape[1] // TILE
    shape = (slots // 2, HEADS, TILE, HEAD_DIM)
    outs = pl.pallas_call(
        unpack_kernel,
        out_shape=[jax.ShapeDtypeStruct(shape, jnp.bfloat16)] * 2,
        in_specs=[pl.BlockSpec(memory_space=pltpu.VMEM)],
        out_specs=[pl.BlockSpec(memory_space=pltpu.HBM)] * 2,
        scratch_shapes=[pltpu.SemaphoreType.DMA((slots,))],
        compiler_params=pltpu.CompilerParams(vmem_limit_bytes=4 * 2**20),
        name="unpack",
    )(packed.reshape(HEADS, slots, TILE, HEAD_DIM))
    return tuple(from_tiles(out) for out in outs)


def solution(mesh):
    teams = plan(mesh)

    def swap(value):
        return lax.all_to_all(value, AXES, 0, 0, axis_index_groups=teams, tiled=True)

    def from_peer(value, by):
        pairs = [pair for at, team in enumerate(teams) for pair in zip(team, teams[(at + by) % len(teams)])]
        return lax.ppermute(value, AXES, pairs)

    def local(query_main, key_main, value_main, query_tan, key_tan, value_tan, positions):
        rows = query_main.shape[0]
        arrays = (query_main, query_tan, key_main, value_main, key_tan, value_tan)
        here = swap(pack(positions, arrays))
        shared = without_queries(here, rows)
        blocks = [here] + [from_peer(shared, by) for by in range(1, len(teams))]
        return unpack(swap(attention(rows, blocks)))

    placed = (P(AXES, None),) * 6 + (P(AXES),)
    return jax.shard_map(
        local,
        mesh=mesh,
        in_specs=placed,
        out_specs=(P(AXES, None), P(AXES, None)),
        check_vma=False,
    )
```

profile of v0, /device:TPU:0, one launch (start us, length us, event | category | flops | bytes accessed | tf_op | source)
XLA Modules:
  0.0 33.1 jit_solution(601022423643872689)
XLA Ops:
  0.6 1.1 %pack.1 = bf16[16,13,8,128]{3,2,1,0:T(8,128)(2,1)S(1)} custom-call(s32[16]{0:T(128)} %positions.1, bf16[2,16,8,128]{3,2,1,0:T(8,128)(2,1)} %bitcast.28, bf16[2,16,8,128]{3,2,1,0:T(8,128)(2,1)} %bitcast.29, bf16[2,16,8,128]{3,2,1,0:T(8,128)(2,1)} %bitcast.30, bf16[2,16,8,128]{3,2,1,0:T(8,128)(2,1)} %bitcast.31, bf16[2,16,8,128]{3,2,1,0:T(8,128)(2,1)} %bitcast.32, ...), custom_call_target="tpu_custom_call" | custom-call | tf_op jit(solution)/shard_map/pack/pallas_call | solution.py:73
  1.7 18.1 %all_to_all.10.whole.refs_0_ = bf16[16,104,128]{2,1,0:T(8,128)(2,1)S(1)} all-to-all(bf16[16,104,128]{2,1,0:T(8,128)(2,1)S(1)} %bitcast.26), channel_id=1, replica_groups={{21,20,17,16,29,28,25,24,5,4,1,0,13,12,9,8},{23,22,19,18,31,30,27,26,7,..., dimensions={0} | all-to-all | bytes 851968 | tf_op jit(solution)/shard_map/all_to_all | solution.py:224
  19.8 0.1 collective-permute-start
  19.9 1.6 %collective-permute-done.refs_1_ = bf16[16,72,128]{2,1,0:T(8,128)(2,1)S(1)} collective-permute-done((bf16[16,72,128]{2,1,0:T(8,128)(2,1)S(1)}, bf16[16,72,128]{2,1,0:T(8,128)(2,1)S(1)}, u32[]{:S(2)}, u32[]{:S(2)}) %collective-permute-start) | collective-permute-done | bytes 294944 | tf_op jit(solution)/shard_map/ppermute | solution.py:228
  21.4 0.7 %attention.1 = bf16[16,32,128]{2,1,0:T(8,128)(2,1)S(1)} custom-call(bf16[16,104,128]{2,1,0:T(8,128)(2,1)S(1)} %all_to_all.10.whole.refs_0_, bf16[16,72,128]{2,1,0:T(8,128)(2,1)S(1)} %collective-permute-done.refs_1_), custom_call_target="tpu_custom_call" | custom-call | tf_op jit(solution)/shard_map/attention/pallas_call | solution.py:182
  22.1 10.4 %all_to_all.11 = bf16[16,32,128]{2,1,0:T(8,128)(2,1)S(1)} all-to-all(bf16[16,32,128]{2,1,0:T(8,128)(2,1)S(1)} %attention.1), channel_id=1, replica_groups={{21,20,17,16,29,28,25,24,5,4,1,0,13,12,9,8},{23,22,19,18,31,30,27,26,7,..., dimensions={0} | all-to-all | bytes 262144 | tf_op jit(solution)/shard_map/all_to_all | solution.py:224
  32.5 0.7 %unpack.1 = (bf16[2,16,8,128]{3,2,1,0:T(8,128)(2,1)}, bf16[2,16,8,128]{3,2,1,0:T(8,128)(2,1)}) custom-call(bf16[16,4,8,128]{3,2,1,0:T(8,128)(2,1)S(1)} %bitcast.27), custom_call_target="tpu_custom_call" | custom-call | tf_op jit(solution)/shard_map/unpack/pallas_call | solution.py:208
  (1 shorter events, 0.0 us)
Async XLA Ops:
  19.8 1.6 %collective-permute-start = (bf16[16,72,128]{2,1,0:T(8,128)(2,1)S(1)}, bf16[16,72,128]{2,1,0:T(8,128)(2,1)S(1)}, u32[]{:S(2)}, u32[]{:S(2)}) collective-permute-start(bf16[16,72,128]{2,1,0:T(8,128)(2,1)S(1)} %shared.1), channel_id=1, source_target_pairs={{21,23},{20,22},{17,19},{16,18},{29,31},{28,30},{25,27},{24,26},{5... | collective-permute-start | bytes 884744 | tf_op jit(solution)/shard_map/ppermute | solution.py:228
where the time goes:
time: 33.4 us; the launch traced here: 33.1 us
  blocking collectives  28.4 us (85%)
  Pallas kernels  2.4 us (7%)
  waiting for transfers between devices  1.57 us (5%)
  between operations  0.66 us (2%)
    all_to_all x2, blocking collectives, swap(): lax.all_to_all(value, AXES, 0, 0, axis_index_groups=teams, tiled=True)  28.4 us
    ppermute x1, waiting for transfers between devices, from_peer(): return lax.ppermute(value, AXES, pairs)  1.57 us
    pallas_call x1, Pallas kernels, pack(): pl.pallas_call(pack_kernel, out_shape=pltpu.VMEM((HEADS, slots, TILE, HEA...  1.05 us
    pallas_call x1, Pallas kernels, unpack(): pl.pallas_call(unpack_kernel, out_shape=[jax.ShapeDtypeStruct(shape, jnp....  0.68 us
  transfers between devices with their start and end apart: 1, of which 1 were waited for; matrix products, arithmetic and copies ran while one was open for 0% of the time, Pallas kernels for 0%

commit v1 on v0

--- a/solution.py
+++ b/solution.py
@@ -110,53 +110,80 @@
     return high.astype(jnp.int32) * 65536 + low.astype(jnp.int32)
 
 
-def attention_kernel(rows, *refs):
+def part(ref, at, rows):
+    return ref[:, at * rows : (at + 1) * rows, :].reshape(-1, HEAD_DIM)
+
+
+def places(ref, rows):
+    lanes = HEAD_DIM * TILE // rows
+    packed = ref[:, ref.shape[1] - TILE :, :].astype(jnp.float32)
+    lane = lax.broadcasted_iota(jnp.int32, packed.shape, 2)
+    parts = [jnp.where(lane // lanes == at, packed, 0.0) for at in range(rows // TILE)]
+    return jnp.stack(parts, axis=1).reshape(-1, HEAD_DIM).astype(jnp.bfloat16)
+
+
+def weights(shape, axis, first, rows):
+    at = lax.broadcasted_iota(jnp.int32, shape, axis) % (HEAD_DIM * TILE // rows)
+    chosen = jnp.where(at == first, 1.0, jnp.where(at == first + 1, 256.0, 0.0))
+    return chosen.astype(jnp.bfloat16)
+
+
+def score(ref, at, queries, query_pair, query_order, rows):
+    keys, key_dot = part(ref, at, rows), part(ref, at + 2, rows)
+    order = places(ref, rows)
+    pieces = [weights((8, HEAD_DIM), 1, first, rows) for first in (2, 0)]
+    key_order = order_of([dot(piece, order, ((1,), (1,))) for piece in pieces])
+    wide_order = jnp.concatenate([query_order] * (keys.shape[0] // HEAD_DIM), axis=1)
+    scores = dot(queries, keys, ((1,), (1,)))
+    scores = jnp.where(key_order[:1] <= wide_order, scores, -1e30)
+    return scores, dot(query_pair, jnp.concatenate([keys, key_dot], axis=1), ((1,), (1,)))
+
+
+def queries_of(own, rows):
+    queries = part(own, 0, rows)
+    return queries, jnp.concatenate([part(own, 1, rows), queries], axis=1)
+
+
+def own_kernel(rows, own, scores_out, tan_out, order_out):
+    own_order = places(own, rows)
+    pieces = [weights((HEAD_DIM, HEAD_DIM), 0, first, rows) for first in (2, 0)]
+    query_order = order_of([dot(own_order, piece, ((1,), (0,))) for piece in pieces])
+    order_out[...] = query_order
+    scores_out[...], tan_out[...] = score(own, 2, *queries_of(own, rows), query_order, rows)
+
+
+def own_scores(rows, here):
+    count = HEADS * rows
+    square = jax.ShapeDtypeStruct((count, count), jnp.float32)
+    return pl.pallas_call(
+        functools.partial(own_kernel, rows),
+        out_shape=(square, square, jax.ShapeDtypeStruct((count, HEAD_DIM), jnp.int32)),
+        in_specs=[pl.BlockSpec(memory_space=pltpu.VMEM)],
+        out_specs=[pl.BlockSpec(memory_space=pltpu.VMEM)] * 3,
+        compiler_params=pltpu.CompilerParams(vmem_limit_bytes=10 * 2**20),
+        name="own_scores",
+    )(here)
+
+
+def attention_kernel(rows, own_raw, own_tan, order, *refs):
     blocks, out = refs[:-1], refs[-1]
     own = blocks[0]
-    count = HEADS * rows
     scale = HEAD_DIM ** (-0.5)
-    lanes = HEAD_DIM * TILE // rows
-
-    def part(ref, at):
-        return ref[:, at * rows : (at + 1) * rows, :].reshape(count, HEAD_DIM)
-
-    def key_part(ref, at):
-        return part(ref, at + 2 if ref is own else at)
-
-    def places(ref):
-        packed = ref[:, ref.shape[1] - TILE :, :].astype(jnp.float32)
-        lane = lax.broadcasted_iota(jnp.int32, packed.shape, 2)
-        parts = [jnp.where(lane // lanes == at, packed, 0.0) for at in range(rows // TILE)]
-        return jnp.stack(parts, axis=1).reshape(count, HEAD_DIM).astype(jnp.bfloat16)
-
-    def weights(shape, axis, first):
-        at = lax.broadcasted_iota(jnp.int32, shape, axis) % lanes
-        chosen = jnp.where(at == first, 1.0, jnp.where(at == first + 1, 256.0, 0.0))
-        return chosen.astype(jnp.bfloat16)
-
-    queries = part(own, 0)
-    query_pair = jnp.concatenate([part(own, 1), queries], axis=1)
-    own_order = places(own)
-    across = (HEAD_DIM, HEAD_DIM)
-    query_order = order_of([dot(own_order, weights(across, 0, first), ((1,), (0,))) for first in (2, 0)])
+    queries, query_pair = queries_of(own, rows)
     state = None
     for start in range(0, len(blocks), 2):
         group = blocks[start : start + 2]
-
-        def keyed(at):
-            return jnp.concatenate([key_part(ref, at) for ref in group], axis=0)
-
-        keys, values, key_dot, value_dot = [keyed(at) for at in range(4)]
-        order = jnp.concatenate([places(ref) for ref in group], axis=0)
-        width = keys.shape[0]
-        down = (8, HEAD_DIM)
-        key_order = order_of([dot(weights(down, 1, first), order, ((1,), (1,))) for first in (2, 0)])
-        wide_order = jnp.concatenate([query_order] * (width // HEAD_DIM), axis=1)
-        visible = key_order[:1] <= wide_order
-        scores = dot(queries, keys, ((1,), (1,)))
-        scores = jnp.where(visible, scores, -1e30)
-        key_pair = jnp.concatenate([keys, key_dot], axis=1)
-        score_tan = dot(query_pair, key_pair, ((1,), (1,)))
+        raw = [
+            (own_raw[...], own_tan[...])
+            if ref is own
+            else score(ref, 0, queries, query_pair, order[...], rows)
+            for ref in group
+        ]
+        scores, score_tan = [jnp.concatenate(each, axis=1) for each in zip(*raw)]
+        values, value_dot = [
+            jnp.concatenate([part(ref, at + 2 if ref is own else at, rows) for ref in group], axis=0)
+            for at in (1, 3)
+        ]
         new_max = jnp.max(scores, axis=1, keepdims=True)
         if state is not None:
             new_max = jnp.maximum(new_max, state[0])
@@ -178,15 +205,16 @@
     out[:, rows:, :] = tangent.astype(jnp.bfloat16).reshape(HEADS, rows, HEAD_DIM)
 
 
-def attention(rows, blocks):
+def attention(rows, raw, blocks):
+    operands = (*raw, *blocks)
     return pl.pallas_call(
         functools.partial(attention_kernel, rows),
         out_shape=jax.ShapeDtypeStruct((HEADS, 2 * rows, HEAD_DIM), jnp.bfloat16),
-        in_specs=[pl.BlockSpec(memory_space=pltpu.VMEM)] * len(blocks),
+        in_specs=[pl.BlockSpec(memory_space=pltpu.VMEM)] * len(operands),
         out_specs=pl.BlockSpec(memory_space=pltpu.VMEM),
-        compiler_params=pltpu.CompilerParams(vmem_limit_bytes=(8 + len(blocks)) * 2**20),
+        compiler_params=pltpu.CompilerParams(vmem_limit_bytes=(10 + len(blocks)) * 2**20),
         name="attention",
-    )(*blocks)
+    )(*operands)
 
 
 def unpack_kernel(packed, *refs):
@@ -233,7 +261,7 @@
         here = swap(pack(positions, arrays))
         shared = without_queries(here, rows)
         blocks = [here] + [from_peer(shared, by) for by in range(1, len(teams))]
-        return unpack(swap(attention(rows, blocks)))
+        return unpack(swap(attention(rows, own_scores(rows, here), blocks)))
 
     placed = (P(AXES, None),) * 6 + (P(AXES),)
     return jax.shard_map(

time: 33.4 us -> 33.3 us (level)
  transfers between devices with their start and end apart: 1 -> 1, of which waited for: 1 -> 1; matrix products, arithmetic and copies ran while one was open for 0% -> 0% of each run, Pallas kernels for 0% -> 1%
where the time goes in v1:
time: 33.3 us; the launch traced here: 33.1 us
  blocking collectives  28.4 us (85%)
  Pallas kernels  2.63 us (8%)
  waiting for transfers between devices  1.26 us (4%)
  between operations  0.66 us (2%)
    all_to_all x2, blocking collectives, swap(): lax.all_to_all(value, AXES, 0, 0, axis_index_groups=teams, tiled=True)  28.4 us
    ppermute x1, waiting for transfers between devices, from_peer(): return lax.ppermute(value, AXES, pairs)  1.26 us
    pallas_call x1, Pallas kernels, pack(): pl.pallas_call(pack_kernel, out_shape=pltpu.VMEM((HEADS, slots, TILE, HEA...  1.05 us
    pallas_call x1, Pallas kernels, unpack(): pl.pallas_call(unpack_kernel, out_shape=[jax.ShapeDtypeStruct(shape, jnp....  0.68 us
  transfers between devices with their start and end apart: 1, of which 1 were waited for; matrix products, arithmetic and copies ran while one was open for 0% of the time, Pallas kernels for 1%

profile of v1, /device:TPU:0, one launch (start us, length us, event | category | flops | bytes accessed | tf_op | source)
XLA Modules:
  0.0 33.1 jit_solution(11592503240138933059)
XLA Ops:
  0.6 1.1 %pack.1 = bf16[16,13,8,128]{3,2,1,0:T(8,128)(2,1)S(1)} custom-call(s32[16]{0:T(128)} %positions.1, bf16[2,16,8,128]{3,2,1,0:T(8,128)(2,1)} %bitcast.28, bf16[2,16,8,128]{3,2,1,0:T(8,128)(2,1)} %bitcast.29, bf16[2,16,8,128]{3,2,1,0:T(8,128)(2,1)} %bitcast.30, bf16[2,16,8,128]{3,2,1,0:T(8,128)(2,1)} %bitcast.31, bf16[2,16,8,128]{3,2,1,0:T(8,128)(2,1)} %bitcast.32, ...), custom_call_target="tpu_custom_call" | custom-call | tf_op jit(solution)/shard_map/pack/pallas_call | solution.py:73
  1.7 18.1 %all_to_all.10.own.whole.refs_0_ = bf16[16,104,128]{2,1,0:T(8,128)(2,1)S(1)} all-to-all(bf16[16,104,128]{2,1,0:T(8,128)(2,1)S(1)} %bitcast.26), channel_id=1, replica_groups={{21,20,17,16,29,28,25,24,5,4,1,0,13,12,9,8},{23,22,19,18,31,30,27,26,7,..., dimensions={0} | all-to-all | bytes 851968 | tf_op jit(solution)/shard_map/all_to_all | solution.py:252
  19.8 0.1 collective-permute-start
  19.9 0.3 own_scores.1
  20.2 1.3 %collective-permute-done.refs_1_ = bf16[16,72,128]{2,1,0:T(8,128)(2,1)S(1)} collective-permute-done((bf16[16,72,128]{2,1,0:T(8,128)(2,1)S(1)}, bf16[16,72,128]{2,1,0:T(8,128)(2,1)S(1)}, u32[]{:S(2)}, u32[]{:S(2)}) %collective-permute-start) | collective-permute-done | bytes 294944 | tf_op jit(solution)/shard_map/ppermute | solution.py:256
  21.4 0.6 %attention.1 = bf16[16,32,128]{2,1,0:T(8,128)(2,1)S(1)} custom-call(f32[256,256]{1,0:T(8,128)S(1)} %get-tuple-element.7.own_raw, f32[256,256]{1,0:T(8,128)S(1)} %get-tuple-element.8.own_tan, s32[256,128]{1,0:T(8,128)S(1)} %get-tuple-element.9.order, bf16[16,104,128]{2,1,0:T(8,128)(2,1)S(1)} %all_to_all.10.own.whole.refs_0_, ...), custom_call_target="tpu_custom_call" | custom-call | tf_op jit(solution)/shard_map/attention/pallas_call | solution.py:210
  22.0 10.4 %all_to_all.11 = bf16[16,32,128]{2,1,0:T(8,128)(2,1)S(1)} all-to-all(bf16[16,32,128]{2,1,0:T(8,128)(2,1)S(1)} %attention.1), channel_id=1, replica_groups={{21,20,17,16,29,28,25,24,5,4,1,0,13,12,9,8},{23,22,19,18,31,30,27,26,7,..., dimensions={0} | all-to-all | bytes 262144 | tf_op jit(solution)/shard_map/all_to_all | solution.py:252
  32.4 0.7 %unpack.1 = (bf16[2,16,8,128]{3,2,1,0:T(8,128)(2,1)}, bf16[2,16,8,128]{3,2,1,0:T(8,128)(2,1)}) custom-call(bf16[16,4,8,128]{3,2,1,0:T(8,128)(2,1)S(1)} %bitcast.27), custom_call_target="tpu_custom_call" | custom-call | tf_op jit(solution)/shard_map/unpack/pallas_call | solution.py:236
  (1 shorter events, 0.0 us)
Async XLA Ops:
  19.8 1.6 %collective-permute-start = (bf16[16,72,128]{2,1,0:T(8,128)(2,1)S(1)}, bf16[16,72,128]{2,1,0:T(8,128)(2,1)S(1)}, u32[]{:S(2)}, u32[]{:S(2)}) collective-permute-start(bf16[16,72,128]{2,1,0:T(8,128)(2,1)S(1)} %shared.1), channel_id=1, source_target_pairs={{21,23},{20,22},{17,19},{16,18},{29,31},{28,30},{25,27},{24,26},{5... | collective-permute-start | bytes 884744 | tf_op jit(solution)/shard_map/ppermute | solution.py:256

commit v2 on v1

--- a/solution.py
+++ b/solution.py
@@ -144,59 +144,54 @@
     return queries, jnp.concatenate([part(own, 1, rows), queries], axis=1)
 
 
-def own_kernel(rows, own, scores_out, tan_out, order_out):
+def sums(scores, score_tan, top, values, value_dot):
+    scale = HEAD_DIM ** (-0.5)
+    expo = jnp.exp2((scores - top) * (scale * LOG2_E))
+    both = dot(expo.astype(jnp.bfloat16), jnp.concatenate([values, value_dot], axis=1), ((1,), (0,)))
+    summed = jnp.concatenate([values, jnp.ones_like(values)], axis=1)
+    moved = dot((expo * score_tan).astype(jnp.bfloat16), summed, ((1,), (0,)))
+    return jnp.sum(expo, axis=1, keepdims=True), both, moved
+
+
+def own_kernel(rows, own, top_out, total_out, both_out, moved_out, order_out):
     own_order = places(own, rows)
     pieces = [weights((HEAD_DIM, HEAD_DIM), 0, first, rows) for first in (2, 0)]
     query_order = order_of([dot(own_order, piece, ((1,), (0,))) for piece in pieces])
+    scores, score_tan = score(own, 2, *queries_of(own, rows), query_order, rows)
+    top = jnp.max(scores, axis=1, keepdims=True)
+    total, both, moved = sums(scores, score_tan, top, part(own, 3, rows), part(own, 5, rows))
     order_out[...] = query_order
-    scores_out[...], tan_out[...] = score(own, 2, *queries_of(own, rows), query_order, rows)
-
-
-def own_scores(rows, here):
+    top_out[...] = jnp.broadcast_to(top, top_out.shape)
+    total_out[...] = jnp.broadcast_to(total, total_out.shape)
+    both_out[...], moved_out[...] = both, moved
+
+
+def own_keys(rows, here):
     count = HEADS * rows
-    square = jax.ShapeDtypeStruct((count, count), jnp.float32)
+    narrow, wide = [jax.ShapeDtypeStruct((count, at * HEAD_DIM), jnp.float32) for at in (1, 2)]
+    order = jax.ShapeDtypeStruct((count, HEAD_DIM), jnp.int32)
     return pl.pallas_call(
         functools.partial(own_kernel, rows),
-        out_shape=(square, square, jax.ShapeDtypeStruct((count, HEAD_DIM), jnp.int32)),
+        out_shape=(narrow, narrow, wide, wide, order),
         in_specs=[pl.BlockSpec(memory_space=pltpu.VMEM)],
-        out_specs=[pl.BlockSpec(memory_space=pltpu.VMEM)] * 3,
+        out_specs=[pl.BlockSpec(memory_space=pltpu.VMEM)] * 5,
         compiler_params=pltpu.CompilerParams(vmem_limit_bytes=10 * 2**20),
-        name="own_scores",
+        name="own_keys",
     )(here)
 
 
-def attention_kernel(rows, own_raw, own_tan, order, *refs):
+def attention_kernel(rows, own, top_in, total_in, both_in, moved_in, order, *refs):
     blocks, out = refs[:-1], refs[-1]
-    own = blocks[0]
     scale = HEAD_DIM ** (-0.5)
     queries, query_pair = queries_of(own, rows)
-    state = None
-    for start in range(0, len(blocks), 2):
-        group = blocks[start : start + 2]
-        raw = [
-            (own_raw[...], own_tan[...])
-            if ref is own
-            else score(ref, 0, queries, query_pair, order[...], rows)
-            for ref in group
-        ]
-        scores, score_tan = [jnp.concatenate(each, axis=1) for each in zip(*raw)]
-        values, value_dot = [
-            jnp.concatenate([part(ref, at + 2 if ref is own else at, rows) for ref in group], axis=0)
-            for at in (1, 3)
-        ]
-        new_max = jnp.max(scores, axis=1, keepdims=True)
-        if state is not None:
-            new_max = jnp.maximum(new_max, state[0])
-        expo = jnp.exp2((scores - new_max) * (scale * LOG2_E))
-        total = jnp.sum(expo, axis=1, keepdims=True)
-        both = dot(expo.astype(jnp.bfloat16), jnp.concatenate([values, value_dot], axis=1), ((1,), (0,)))
-        summed = jnp.concatenate([values, jnp.ones_like(values)], axis=1)
-        moved = dot((expo * score_tan).astype(jnp.bfloat16), summed, ((1,), (0,)))
-        if state is not None:
-            shrink = jnp.exp2((state[0] - new_max) * (scale * LOG2_E))
-            total, both, moved = [new + old * shrink for new, old in zip((total, both, moved), state[1:])]
-        state = (new_max, total, both, moved)
-    _, total, both, moved = state
+    top, total, both, moved = top_in[...][:, :1], total_in[...][:, :1], both_in[...], moved_in[...]
+    for ref in blocks:
+        scores, score_tan = score(ref, 0, queries, query_pair, order[...], rows)
+        new_top = jnp.maximum(jnp.max(scores, axis=1, keepdims=True), top)
+        new = sums(scores, score_tan, new_top, part(ref, 1, rows), part(ref, 3, rows))
+        shrink = jnp.exp2((top - new_top) * (scale * LOG2_E))
+        total, both, moved = [now + old * shrink for now, old in zip(new, (total, both, moved))]
+        top = new_top
     inverse = 1.0 / total
     mixed = both[:, :HEAD_DIM] * inverse
     weighted, mass = moved[:, :HEAD_DIM], moved[:, HEAD_DIM:]
@@ -205,14 +200,14 @@
     out[:, rows:, :] = tangent.astype(jnp.bfloat16).reshape(HEADS, rows, HEAD_DIM)
 
 
-def attention(rows, raw, blocks):
-    operands = (*raw, *blocks)
+def attention(rows, here, others):
+    operands = (here, *own_keys(rows, here), *others)
     return pl.pallas_call(
         functools.partial(attention_kernel, rows),
         out_shape=jax.ShapeDtypeStruct((HEADS, 2 * rows, HEAD_DIM), jnp.bfloat16),
         in_specs=[pl.BlockSpec(memory_space=pltpu.VMEM)] * len(operands),
         out_specs=pl.BlockSpec(memory_space=pltpu.VMEM),
-        compiler_params=pltpu.CompilerParams(vmem_limit_bytes=(10 + len(blocks)) * 2**20),
+        compiler_params=pltpu.CompilerParams(vmem_limit_bytes=(10 + len(others)) * 2**20),
         name="attention",
     )(*operands)
 
@@ -260,8 +255,8 @@
         arrays = (query_main, query_tan, key_main, value_main, key_tan, value_tan)
         here = swap(pack(positions, arrays))
         shared = without_queries(here, rows)
-        blocks = [here] + [from_peer(shared, by) for by in range(1, len(teams))]
-        return unpack(swap(attention(rows, own_scores(rows, here), blocks)))
+        others = [from_peer(shared, by) for by in range(1, len(teams))]
+        return unpack(swap(attention(rows, here, others)))
 
     placed = (P(AXES, None),) * 6 + (P(AXES),)
     return jax.shard_map(

time: 33.3 us -> 33.4 us (level)
  transfers between devices with their start and end apart: 1 -> 1, of which waited for: 1 -> 1; matrix products, arithmetic and copies ran while one was open for 0% -> 0% of each run, Pallas kernels for 1% -> 2%
where the time goes in v2:
time: 33.4 us; the launch traced here: 33.1 us
  blocking collectives  28.4 us (85%)
  Pallas kernels  2.91 us (9%)
  waiting for transfers between devices  1.04 us (3%)
  between operations  0.66 us (2%)
    all_to_all x2, blocking collectives, swap(): lax.all_to_all(value, AXES, 0, 0, axis_index_groups=teams, tiled=True)  28.4 us
    pallas_call x1, Pallas kernels, pack(): pl.pallas_call(pack_kernel, out_shape=pltpu.VMEM((HEADS, slots, TILE, HEA...  1.05 us
    ppermute x1, waiting for transfers between devices, from_peer(): return lax.ppermute(value, AXES, pairs)  1.04 us
    pallas_call x1, Pallas kernels, unpack(): pl.pallas_call(unpack_kernel, out_shape=[jax.ShapeDtypeStruct(shape, jnp....  0.68 us
  transfers between devices with their start and end apart: 1, of which 1 were waited for; matrix products, arithmetic and copies ran while one was open for 0% of the time, Pallas kernels for 2%

profile of v2, /device:TPU:0, one launch (start us, length us, event | category | flops | bytes accessed | tf_op | source)
XLA Modules:
  0.0 33.1 jit_solution(16743006998114251316)
XLA Ops:
  0.6 1.1 %pack.1 = bf16[16,13,8,128]{3,2,1,0:T(8,128)(2,1)S(1)} custom-call(s32[16]{0:T(128)} %positions.1, bf16[2,16,8,128]{3,2,1,0:T(8,128)(2,1)} %bitcast.28, bf16[2,16,8,128]{3,2,1,0:T(8,128)(2,1)} %bitcast.29, bf16[2,16,8,128]{3,2,1,0:T(8,128)(2,1)} %bitcast.30, bf16[2,16,8,128]{3,2,1,0:T(8,128)(2,1)} %bitcast.31, bf16[2,16,8,128]{3,2,1,0:T(8,128)(2,1)} %bitcast.32, ...), custom_call_target="tpu_custom_call" | custom-call | tf_op jit(solution)/shard_map/pack/pallas_call | solution.py:73
  1.7 18.1 %all_to_all.10.own.whole = bf16[16,104,128]{2,1,0:T(8,128)(2,1)S(1)} all-to-all(bf16[16,104,128]{2,1,0:T(8,128)(2,1)S(1)} %bitcast.26), channel_id=1, replica_groups={{21,20,17,16,29,28,25,24,5,4,1,0,13,12,9,8},{23,22,19,18,31,30,27,26,7,..., dimensions={0} | all-to-all | bytes 851968 | tf_op jit(solution)/shard_map/all_to_all | solution.py:247
  19.8 0.1 collective-permute-start
  19.9 0.5 %own_keys.1 = (f32[256,128]{1,0:T(8,128)S(1)}, f32[256,128]{1,0:T(8,128)S(1)}, f32[256,256]{1,0:T(8,128)S(1)}, f32[256,256]{1,0:T(8,128)S(1)}, s32[256,128]{1,0:T(8,128)S(1)}) custom-call(bf16[16,104,128]{2,1,0:T(8,128)(2,1)S(1)} %all_to_all.10.own.whole), custom_call_target="tpu_custom_call" | custom-call | tf_op jit(solution)/shard_map/own_keys/pallas_call | solution.py:173
  20.4 1.0 %collective-permute-done.refs_0_ = bf16[16,72,128]{2,1,0:T(8,128)(2,1)S(1)} collective-permute-done((bf16[16,72,128]{2,1,0:T(8,128)(2,1)S(1)}, bf16[16,72,128]{2,1,0:T(8,128)(2,1)S(1)}, u32[]{:S(2)}, u32[]{:S(2)}) %collective-permute-start) | collective-permute-done | bytes 294944 | tf_op jit(solution)/shard_map/ppermute | solution.py:251
  21.4 0.6 %attention.1 = bf16[16,32,128]{2,1,0:T(8,128)(2,1)S(1)} custom-call(bf16[16,104,128]{2,1,0:T(8,128)(2,1)S(1)} %all_to_all.10.own.whole, f32[256,128]{1,0:T(8,128)S(1)} %get-tuple-element.9.top_in, f32[256,128]{1,0:T(8,128)S(1)} %get-tuple-element.10.total_in, f32[256,256]{1,0:T(8,128)S(1)} %get-tuple-element.11.both_in, ...), custom_call_target="tpu_custom_call" | custom-call | tf_op jit(solution)/shard_map/attention/pallas_call | solution.py:205
  22.1 10.4 %all_to_all.11 = bf16[16,32,128]{2,1,0:T(8,128)(2,1)S(1)} all-to-all(bf16[16,32,128]{2,1,0:T(8,128)(2,1)S(1)} %attention.1), channel_id=1, replica_groups={{21,20,17,16,29,28,25,24,5,4,1,0,13,12,9,8},{23,22,19,18,31,30,27,26,7,..., dimensions={0} | all-to-all | bytes 262144 | tf_op jit(solution)/shard_map/all_to_all | solution.py:247
  32.4 0.7 %unpack.1 = (bf16[2,16,8,128]{3,2,1,0:T(8,128)(2,1)}, bf16[2,16,8,128]{3,2,1,0:T(8,128)(2,1)}) custom-call(bf16[16,4,8,128]{3,2,1,0:T(8,128)(2,1)S(1)} %bitcast.27), custom_call_target="tpu_custom_call" | custom-call | tf_op jit(solution)/shard_map/unpack/pallas_call | solution.py:231
  (1 shorter events, 0.0 us)
Async XLA Ops:
  19.8 1.6 %collective-permute-start = (bf16[16,72,128]{2,1,0:T(8,128)(2,1)S(1)}, bf16[16,72,128]{2,1,0:T(8,128)(2,1)S(1)}, u32[]{:S(2)}, u32[]{:S(2)}) collective-permute-start(bf16[16,72,128]{2,1,0:T(8,128)(2,1)S(1)} %shared.1), channel_id=1, source_target_pairs={{21,23},{20,22},{17,19},{16,18},{29,31},{28,30},{25,27},{24,26},{5... | collective-permute-start | bytes 884744 | tf_op jit(solution)/shard_map/ppermute | solution.py:251

commit v3 on v1

--- a/solution.py
+++ b/solution.py
@@ -44,14 +44,17 @@
     arrays, (out, here, sems) = refs[:ARRAYS], refs[ARRAYS:]
     row_tiles = arrays[0].shape[0]
     last = ARRAYS * row_tiles
-    load = pltpu.make_async_copy(positions, here, sems.at[last])
+    load = pltpu.make_async_copy(positions, here, sems.at[2 * last])
     load.start()
     copies = []
     for at, array in enumerate(arrays):
         for tile in range(row_tiles):
             slot = at * row_tiles + tile
-            copies.append(pltpu.make_async_copy(array.at[tile], out.at[:, slot], sems.at[slot]))
-            copies[-1].start()
+            for half in range(2):
+                heads = pl.ds(half * HEADS // 2, HEADS // 2)
+                sem = sems.at[len(copies)]
+                copies.append(pltpu.make_async_copy(array.at[tile, heads], out.at[heads, slot], sem))
+                copies[-1].start()
     token = lax.broadcasted_iota(jnp.int32, (TILE, HEAD_DIM), 0)
     lane = lax.broadcasted_iota(jnp.int32, (TILE, HEAD_DIM), 1)
     token = token + lane // (HEAD_DIM // row_tiles) * TILE
@@ -77,7 +80,7 @@
         out_specs=pl.BlockSpec(memory_space=pltpu.VMEM),
         scratch_shapes=[
             pltpu.SMEM(positions.shape, jnp.int32),
-            pltpu.SemaphoreType.DMA((slots,)),
+            pltpu.SemaphoreType.DMA((2 * slots - 1,)),
         ],
         compiler_params=pltpu.CompilerParams(vmem_limit_bytes=56 * 2**20),
         name="pack",

time: 33.3 us -> 33.5 us (level)
  no operation moved by 1% of the time
where the time goes in v3:
time: 33.5 us; the launch traced here: 33.2 us
  blocking collectives  28.4 us (85%)
  Pallas kernels  2.74 us (8%)
  waiting for transfers between devices  1.26 us (4%)
  between operations  0.66 us (2%)
    all_to_all x2, blocking collectives, swap(): lax.all_to_all(value, AXES, 0, 0, axis_index_groups=teams, tiled=True)  28.4 us
    ppermute x1, waiting for transfers between devices, from_peer(): return lax.ppermute(value, AXES, pairs)  1.26 us
    pallas_call x1, Pallas kernels, pack(): pl.pallas_call(pack_kernel, out_shape=pltpu.VMEM((HEADS, slots, TILE, HEA...  1.16 us
    pallas_call x1, Pallas kernels, unpack(): pl.pallas_call(unpack_kernel, out_shape=[jax.ShapeDtypeStruct(shape, jnp....  0.68 us
  transfers between devices with their start and end apart: 1, of which 1 were waited for; matrix products, arithmetic and copies ran while one was open for 0% of the time, Pallas kernels for 1%

profile of v3, /device:TPU:0, one launch (start us, length us, event | category | flops | bytes accessed | tf_op | source)
XLA Modules:
  0.0 33.2 jit_solution(10517642464200106986)
XLA Ops:
  0.6 1.2 %pack.1 = bf16[16,13,8,128]{3,2,1,0:T(8,128)(2,1)S(1)} custom-call(s32[16]{0:T(128)} %positions.1, bf16[2,16,8,128]{3,2,1,0:T(8,128)(2,1)} %bitcast.28, bf16[2,16,8,128]{3,2,1,0:T(8,128)(2,1)} %bitcast.29, bf16[2,16,8,128]{3,2,1,0:T(8,128)(2,1)} %bitcast.30, bf16[2,16,8,128]{3,2,1,0:T(8,128)(2,1)} %bitcast.31, bf16[2,16,8,128]{3,2,1,0:T(8,128)(2,1)} %bitcast.32, ...), custom_call_target="tpu_custom_call" | custom-call | tf_op jit(solution)/shard_map/pack/pallas_call | solution.py:76
  1.8 18.1 %all_to_all.10.own.whole.refs_0_ = bf16[16,104,128]{2,1,0:T(8,128)(2,1)S(1)} all-to-all(bf16[16,104,128]{2,1,0:T(8,128)(2,1)S(1)} %bitcast.26), channel_id=1, replica_groups={{21,20,17,16,29,28,25,24,5,4,1,0,13,12,9,8},{23,22,19,18,31,30,27,26,7,..., dimensions={0} | all-to-all | bytes 851968 | tf_op jit(solution)/shard_map/all_to_all | solution.py:255
  19.9 0.1 collective-permute-start
  20.0 0.3 own_scores.1
  20.3 1.3 %collective-permute-done.refs_1_ = bf16[16,72,128]{2,1,0:T(8,128)(2,1)S(1)} collective-permute-done((bf16[16,72,128]{2,1,0:T(8,128)(2,1)S(1)}, bf16[16,72,128]{2,1,0:T(8,128)(2,1)S(1)}, u32[]{:S(2)}, u32[]{:S(2)}) %collective-permute-start) | collective-permute-done | bytes 294944 | tf_op jit(solution)/shard_map/ppermute | solution.py:259
  21.6 0.6 %attention.1 = bf16[16,32,128]{2,1,0:T(8,128)(2,1)S(1)} custom-call(f32[256,256]{1,0:T(8,128)S(1)} %get-tuple-element.7.own_raw, f32[256,256]{1,0:T(8,128)S(1)} %get-tuple-element.8.own_tan, s32[256,128]{1,0:T(8,128)S(1)} %get-tuple-element.9.order, bf16[16,104,128]{2,1,0:T(8,128)(2,1)S(1)} %all_to_all.10.own.whole.refs_0_, ...), custom_call_target="tpu_custom_call" | custom-call | tf_op jit(solution)/shard_map/attention/pallas_call | solution.py:213
  22.1 10.4 %all_to_all.11 = bf16[16,32,128]{2,1,0:T(8,128)(2,1)S(1)} all-to-all(bf16[16,32,128]{2,1,0:T(8,128)(2,1)S(1)} %attention.1), channel_id=1, replica_groups={{21,20,17,16,29,28,25,24,5,4,1,0,13,12,9,8},{23,22,19,18,31,30,27,26,7,..., dimensions={0} | all-to-all | bytes 262144 | tf_op jit(solution)/shard_map/all_to_all | solution.py:255
  32.5 0.7 %unpack.1 = (bf16[2,16,8,128]{3,2,1,0:T(8,128)(2,1)}, bf16[2,16,8,128]{3,2,1,0:T(8,128)(2,1)}) custom-call(bf16[16,4,8,128]{3,2,1,0:T(8,128)(2,1)S(1)} %bitcast.27), custom_call_target="tpu_custom_call" | custom-call | tf_op jit(solution)/shard_map/unpack/pallas_call | solution.py:239
  (1 shorter events, 0.0 us)
Async XLA Ops:
  19.9 1.6 %collective-permute-start = (bf16[16,72,128]{2,1,0:T(8,128)(2,1)S(1)}, bf16[16,72,128]{2,1,0:T(8,128)(2,1)S(1)}, u32[]{:S(2)}, u32[]{:S(2)}) collective-permute-start(bf16[16,72,128]{2,1,0:T(8,128)(2,1)S(1)} %shared.1), channel_id=1, source_target_pairs={{21,23},{20,22},{17,19},{16,18},{29,31},{28,30},{25,27},{24,26},{5... | collective-permute-start | bytes 884744 | tf_op jit(solution)/shard_map/ppermute | solution.py:259
